TPU v7x, 256 devices: a whole 4x4x8 slice. The times are simulated.
256 devices in a mesh: dp: 32 (over x, z), seq: 8 (over y, core).
Axes of the slice: x: 4, y: 4, z: 8, core: 2. Of those that a mesh axis runs over, the one named last changes fastest.
Arguments:
- pixels: bfloat16 [32768, 1176], P(('dp', 'seq')), may hold values from -6 to 6
- patch_weight: bfloat16 [1176, 1280], replicated, may hold values from -0.1875 to 0.1875
- ln_gain: float32 [1280], replicated, may hold values from 0.1 to 1.9
- ln_bias: float32 [1280], replicated, may hold values from -1.5 to 1.5
- qkv_weight: bfloat16 [1280, 3840], P('dp'), may hold values from -4 to 4
- qkv_bias: float32 [3840], replicated, may hold values from -2.5 to 2.5
- out_weight: bfloat16 [1280, 1280], P('dp'), may hold values from -0.15625 to 0.15625
- out_bias: float32 [1280], replicated, may hold values from -1.5 to 1.5
- offsets: int32 [32, 3], P('dp'), may hold values from 0 to 854, as said below
- widths: int32 [32, 3], P('dp'), may hold values from 16 to 64
Outputs:
- encoded: bfloat16 [32768, 1280], P(('dp', 'seq'))
Inputs may be any that keep to these rules, and one draw needn't show every extreme that they name: In every group the first offset is 0 and offsets rise; every image holds 170 or more tokens and the last image ends at position 1024; in some group the last image holds exactly 170 tokens.
All inputs are finite; a program needn't handle non-finite values.
Results may differ from a plain program's by a relative error of at most 0.012.
Values may be sent and summed in bfloat16 or wider, within the bound.
No kernel may reach another device: no remote copies, remote signals or barrier semaphores. Data moves between devices by JAX's collectives and lax.ppermute only.
A program may use at most 64 MiB of HBM per device.

v0:
```python
import jax
import jax.numpy as jnp
from jax import lax
from jax.sharding import PartitionSpec as P

HEADS = 16
HDIM = 80


def image_lookup(positions, starts):
    return jnp.sum((positions[:, None] >= starts[None, :]).astype(jnp.int32), axis=1) - 1


def rotation_tables(positions, starts, image_widths, head_size):
    image_index = image_lookup(positions, starts)
    onehot = (image_index[:, None] == jnp.arange(starts.shape[0], dtype=jnp.int32)[None, :]).astype(
        jnp.int32
    )
    first_position = jnp.sum(onehot * starts[None, :], axis=1)
    across = jnp.sum(onehot * image_widths[None, :], axis=1)
    within = positions - first_position
    row_index = within // across
    column_index = within - row_index * across
    quarter = head_size // 4
    inverse = 1.0 / 10000.0 ** (jnp.arange(quarter, dtype=jnp.float32) * 2.0 / (head_size // 2))
    angles = jnp.concatenate(
        [
            row_index.astype(jnp.float32)[:, None] * inverse[None, :],
            column_index.astype(jnp.float32)[:, None] * inverse[None, :],
        ],
        axis=1,
    )
    angles = jnp.concatenate([angles, angles], axis=1)
    return (jnp.cos(angles), jnp.sin(angles), image_index)


def rotate_heads(values, cosine, sine_table, head_size):
    half_size = head_size // 2
    turned = jnp.concatenate([-values[..., half_size:], values[..., :half_size]], axis=-1)
    return values * cosine[:, None, :] + turned * sine_table[:, None, :]


def layer_norm(embedded, ln_gain, ln_bias):
    values = embedded.astype(jnp.float32)
    center = values - jnp.mean(values, axis=-1, keepdims=True)
    variance = jnp.mean(center * center, axis=-1, keepdims=True)
    return (center * lax.rsqrt(variance + 1e-06) * ln_gain + ln_bias).astype(jnp.bfloat16)


def block_length(count):
    length = min(count, 512)
    while count % length:
        length -= 1
    return length


def attend_block(state, queries3, key_block, value_block, query_image, key_image, score_scale):
    running_max, running_total, accum = state
    count = key_block.shape[0]
    scores = (
        jnp.einsum(
            "qhd,khd->hqk",
            queries3,
            key_block.reshape(count, HEADS, HDIM),
            preferred_element_type=jnp.float32,
        )
        * score_scale
    )
    allowed = (query_image[:, None] == key_image[None, :])[None]
    scores = jnp.where(allowed, scores, -1e30)
    new_max = jnp.maximum(running_max, jnp.max(scores, axis=-1))
    weights = jnp.where(allowed, jnp.exp(scores - new_max[..., None]), 0.0)
    factor = jnp.exp(running_max - new_max)
    running_total = running_total * factor + jnp.sum(weights, axis=-1)
    part_sum = jnp.einsum(
        "hqk,khd->qhd",
        weights.astype(jnp.bfloat16),
        value_block.reshape(count, HEADS, HDIM),
        preferred_element_type=jnp.float32,
    )
    accum = accum * factor.T[:, :, None] + part_sum
    return (new_max, running_total, accum)


def per_device(
    pixels,
    patch_weight,
    ln_gain,
    ln_bias,
    qkv_weight,
    qkv_bias,
    out_weight,
    out_bias,
    offsets,
    widths,
):
    local_pixels = lax.all_to_all(pixels, "dp", split_axis=0, concat_axis=0, tiled=True)
    tok_rows = local_pixels.shape[0]
    dmodel = patch_weight.shape[1]
    score_scale = HDIM ** (-0.5)
    embedded = jnp.dot(local_pixels, patch_weight, preferred_element_type=jnp.float32).astype(
        jnp.bfloat16
    )
    normed = layer_norm(embedded, ln_gain, ln_bias)
    columns = normed
    projected = (
        jnp.dot(
            columns,
            lax.all_gather(qkv_weight, "dp", axis=0, tiled=True),
            preferred_element_type=jnp.float32,
        )
        + qkv_bias
    )
    starts = offsets[0]
    image_widths = widths[0]
    positions = lax.axis_index("seq") * tok_rows + jnp.arange(tok_rows, dtype=jnp.int32)
    cosine, sine_table, query_image = rotation_tables(positions, starts, image_widths, HDIM)
    queries = (
        rotate_heads(projected[:, :dmodel].reshape(tok_rows, HEADS, HDIM), cosine, sine_table, HDIM)
        .reshape(tok_rows, dmodel)
        .astype(jnp.bfloat16)
    )
    key_rows = (
        rotate_heads(
            projected[:, dmodel : 2 * dmodel].reshape(tok_rows, HEADS, HDIM),
            cosine,
            sine_table,
            HDIM,
        )
        .reshape(tok_rows, dmodel)
        .astype(jnp.bfloat16)
    )
    values = projected[:, 2 * dmodel :].astype(jnp.bfloat16)
    queries3 = queries.reshape(tok_rows, HEADS, HDIM)
    initial = (
        jnp.full((HEADS, tok_rows), -1e30, jnp.float32),
        jnp.zeros((HEADS, tok_rows), jnp.float32),
        jnp.zeros((tok_rows, HEADS, HDIM), jnp.float32),
    )
    piece_keys = lax.all_gather(key_rows, "seq", axis=0, tiled=True)
    piece_values = lax.all_gather(values, "seq", axis=0, tiled=True)
    count = piece_keys.shape[0]
    length = block_length(count)

    def one_block(block_index, inner):
        first_row = block_index * length
        key_block = lax.dynamic_slice_in_dim(piece_keys, first_row, length, 0)
        value_block = lax.dynamic_slice_in_dim(piece_values, first_row, length, 0)
        key_image = image_lookup(first_row + jnp.arange(length, dtype=jnp.int32), starts)
        return attend_block(
            inner, queries3, key_block, value_block, query_image, key_image, score_scale
        )

    final_state = lax.fori_loop(0, count // length, one_block, initial)
    attended = (
        (final_state[2] / final_state[1].T[:, :, None])
        .reshape(tok_rows, dmodel)
        .astype(jnp.bfloat16)
    )
    columns = attended
    mixed = jnp.dot(
        columns,
        lax.all_gather(out_weight, "dp", axis=0, tiled=True),
        preferred_element_type=jnp.float32,
    )
    return (embedded.astype(jnp.float32) + mixed + out_bias).astype(jnp.bfloat16)


def solution(mesh):
    in_specs = (
        P(("dp", "seq"), None),
        P(),
        P(),
        P(),
        P("dp", None),
        P(),
        P("dp", None),
        P(),
        P("dp", None),
        P("dp", None),
    )
    out_specs = P(("dp", "seq"), None)
    return jax.shard_map(
        per_device, mesh=mesh, in_specs=in_specs, out_specs=out_specs, check_vma=False
    )
```

profile of v0, /device:TPU:8, one launch (start us, length us, event | category | flops | bytes accessed | tf_op | source)
XLA Modules:
  0.0 290.6 jit_solution(15201041775588603741)
XLA Ops:
  6.5 0.0 copy-start
  6.5 0.0 all-gather.5.cloned.1.call-start
  6.5 0.7 all-gather.5.cloned.1.call-update
  7.3 1.3 copy.27
  8.6 0.8 all_to_all.8
  9.4 11.4 %all-to-all-start = ((bf16[32,4,1176]{2,1,0:T(4,128)(2,1)}), bf16[32,4,1176]{2,1,0:T(4,128)(2,1)}, u32[]{:S(2)}, u32[]{:S(2)}) async-start(bf16[32,4,1176]{2,1,0:T(4,128)(2,1)} %all_to_all.8), calls=%async_computation | async-start | bytes 655360 | tf_op jit(solution)/shard_map/all_to_all | solution.py:97
  20.8 0.0 all-gather.7.cloned.1.call-start
  20.9 0.7 convert_reduce_fusion.1
  21.6 0.8 select_reduce_fusion.1
  22.4 0.1 fusion.26
  22.6 0.1 broadcast_multiply_fusion.1
  22.6 0.2 fusion.25
  22.8 0.9 mul.198
  23.7 2.2 copy.28
  25.9 8.5 %all-to-all-done = bf16[32,4,1176]{2,1,0:T(4,128)(2,1)} async-done(((bf16[32,4,1176]{2,1,0:T(4,128)(2,1)}), bf16[32,4,1176]{2,1,0:T(4,128)(2,1)}, u32[]{:S(2)}, u32[]{:S(2)}) %all-to-all-start) | async-done | bytes 301088 | tf_op jit(solution)/shard_map/all_to_all | solution.py:97
  34.4 1.1 all_to_all.10
  35.5 0.0 copy-done
  35.5 0.7 fusion.28
  36.2 0.0 copy-start.2
  36.2 0.8 copy-done.2
  37.1 0.2 multiply_reduce_fusion
  37.3 81.0 %all-gather.5.cloned.1.call-done = bf16[1280,3840]{1,0:T(8,128)(2,1)} async-done(((bf16[40,3840]{1,0:T(8,128)(2,1)}), bf16[1280,3840]{1,0:T(8,128)(2,1)}) %all-gather.5.cloned.1.call-update) | async-done | bytes 9830416 | tf_op jit(solution)/shard_map/all_gather | solution.py:109
  118.3 0.0 copy-done.4
  118.3 5.5 %convolution_add_fusion = f32[128,3840]{1,0:T(8,128)S(1)} fusion(bf16[1280,3840]{1,0:T(8,128)(2,1)} %all-gather.5.cloned.1.call-done, f32[3840]{0:T(1024)S(1)} %copy-done.7, f32[128,1280]{1,0:T(8,128)} %copy-done.2, f32[1280]{0:T(1024)S(1)} %copy-done.4, f32[1280]{0:T(1024)S(1)} %copy-done.5, f32[128]{0:T(128)S(1)} %add_rsqrt_fusion, ...), kind=kOutput, calls=%fused_computation.24 | convolution fusion | flops 1259601920 | bytes 12478464 | tf_op jit(solution)/shard_map/dot_general | solution.py:107
  123.8 1.3 copy-done.3
  125.1 1.1 fusion.27
  126.3 2.1 copy.29
  128.4 2.2 copy.32
  130.6 1.4 slice_negate_fusion
  131.9 1.2 maximum_multiply_fusion.1
  133.1 2.2 copy.30
  135.2 2.2 copy.33
  137.4 2.9 add_convert_fusion
  140.3 0.0 all-gather.7.cloned.1.call-update
  140.3 0.0 all-gather.9.cloned.1.call-start
  140.4 1.8 slice.41
  142.2 0.0 all-gather.9.cloned.1.call-update
  142.2 0.0 all-gather.11.cloned.1.call-start
  142.3 0.5 all-gather.11.cloned.1.call-update
  142.8 1.2 copy.34
  144.0 21.3 %all-gather.7.cloned.1.call-done = bf16[1024,1280]{1,0:T(8,128)(2,1)} async-done(((bf16[128,1280]{1,0:T(8,128)(2,1)}), bf16[1024,1280]{1,0:T(8,128)(2,1)}) %all-gather.7.cloned.1.call-update) | async-done | bytes 2621456 | tf_op jit(solution)/shard_map/all_gather | solution.py:140
  165.3 31.1 %all-gather.9.cloned.1.call-done = bf16[1024,1280]{1,0:T(8,128)(2,1)} async-done(((bf16[128,1280]{1,0:T(8,128)(2,1)}), bf16[1024,1280]{1,0:T(8,128)(2,1)}) %all-gather.9.cloned.1.call-update) | async-done | bytes 2621456 | tf_op jit(solution)/shard_map/all_gather | solution.py:141
  196.5 37.7 %while.20 = (s32[]{:T(128)}, f32[16,128]{1,0:T(8,128)S(1)}, f32[16,128]{1,0:T(8,128)S(1)}, f32[128,16,80]{0,2,1:T(8,128)}, s32[128]{0:T(128)S(1)}, /*index=5*/s3...) while((s32[]{:T(128)}, f32[16,128]{1,0:T(8,128)S(1)}, ...), condition=%wide.region_9.10_spmd.clone, body=%wide.region_5.9_spmd.clone.sunk | while | flops 349750272 | bytes 44511972 | solution.py:154
  196.5 3.5 %constant_dynamic-slice_fusion.3 = (bf16[512,1280]{1,0:T(8,128)(2,1)}, bf16[512,1280]{1,0:T(8,128)(2,1)}) fusion(bf16[1024,1280]{1,0:T(8,128)(2,1)} %get-tuple-element.432, s32[]{:T(128)S(6)} %select_n.85, bf16[1024,1280]{1,0:T(8,128)(2,1)} %get-tuple-element.430), kind=kLoop, calls=%fused_computation.19.clone.1 | loop fusion | bytes 5242884 | tf_op jit(solution)/shard_map/while/body/eval_jaxpr/dynamic_slice | solution.py:148
  199.9 2.4 copy.42
  202.4 0.1 convert_reduce_fusion.3
  202.5 0.1 broadcast_compare_fusion.2
  202.6 4.3 %fusion.50 = (f32[16,128]{1,0:T(8,128)S(1)}, f32[16,512,128]{2,1,0:T(8,128)}) fusion(pred[128,512]{0,1:T(8,128)(4,1)S(1)} %broadcast_compare_fusion.2, bf16[512,16,80]{0,2,1:T(8,128)(2,1)} %bitcast.64, bf16[128,16,80]{0,2,1:T(8,128)(2,1)S(1)} %get-tuple-element.431), kind=kOutput, calls=%fused_computation.2.clone.1 | convolution fusion | flops 170915840 | bytes 5906432 | tf_op jit(solution)/shard_map/while/body/eval_jaxpr/qhd,khd->hqk/dot_general | solution.py:61
  206.9 2.4 copy.43
  209.3 4.8 %fusion.54 = f32[128,16,80]{0,2,1:T(8,128)} fusion(bf16[512,16,80]{0,2,1:T(8,128)(2,1)} %bitcast.65, f32[16,512,128]{2,1,0:T(8,128)} %get-tuple-element.395, f32[16,128]{1,0:T(8,128)S(1)} %get-tuple-element.425, pred[128,512]{0,1:T(8,128)(4,1)S(1)} %broadcast_compare_fusion.2, f32[128,16,80]{0,2,1:T(8,128)} %get-tuple-element.414, ...), kind=kOutput, calls=%fused_computation.8.clone.1 | convolution fusion | flops 173506560 | bytes 6897665 | tf_op jit(solution)/shard_map/while/body/eval_jaxpr/hqk,khd->qhd/dot_general | solution.py:75
  214.2 0.0 copy-done.1
  214.2 1.0 fusion.52
  215.3 3.5 %constant_dynamic-slice_fusion.3 = (bf16[512,1280]{1,0:T(8,128)(2,1)}, bf16[512,1280]{1,0:T(8,128)(2,1)}) fusion(bf16[1024,1280]{1,0:T(8,128)(2,1)} %get-tuple-element.432, s32[]{:T(128)S(6)} %select_n.85, bf16[1024,1280]{1,0:T(8,128)(2,1)} %get-tuple-element.430), kind=kLoop, calls=%fused_computation.19.clone.1 | loop fusion | bytes 5242884 | tf_op jit(solution)/shard_map/while/body/eval_jaxpr/dynamic_slice | solution.py:148
  218.7 2.4 copy.42
  221.2 0.1 convert_reduce_fusion.3
  221.3 0.1 broadcast_compare_fusion.2
  221.4 4.3 %fusion.50 = (f32[16,128]{1,0:T(8,128)S(1)}, f32[16,512,128]{2,1,0:T(8,128)}) fusion(pred[128,512]{0,1:T(8,128)(4,1)S(1)} %broadcast_compare_fusion.2, bf16[512,16,80]{0,2,1:T(8,128)(2,1)} %bitcast.64, bf16[128,16,80]{0,2,1:T(8,128)(2,1)S(1)} %get-tuple-element.431), kind=kOutput, calls=%fused_computation.2.clone.1 | convolution fusion | flops 170915840 | bytes 5906432 | tf_op jit(solution)/shard_map/while/body/eval_jaxpr/qhd,khd->hqk/dot_general | solution.py:61
  225.7 2.4 copy.43
  228.1 5.0 %fusion.54 = f32[128,16,80]{0,2,1:T(8,128)} fusion(bf16[512,16,80]{0,2,1:T(8,128)(2,1)} %bitcast.65, f32[16,512,128]{2,1,0:T(8,128)} %get-tuple-element.395, f32[16,128]{1,0:T(8,128)S(1)} %get-tuple-element.425, pred[128,512]{0,1:T(8,128)(4,1)S(1)} %broadcast_compare_fusion.2, f32[128,16,80]{0,2,1:T(8,128)} %get-tuple-element.414, ...), kind=kOutput, calls=%fused_computation.8.clone.1 | convolution fusion | flops 173506560 | bytes 6897665 | tf_op jit(solution)/shard_map/while/body/eval_jaxpr/hqk,khd->qhd/dot_general | solution.py:75
  233.1 0.0 copy-done.1
  233.1 1.0 fusion.52
  234.2 1.1 divide_convert_fusion
  235.3 45.3 %all-gather.11.cloned.1.call-done = bf16[1280,1280]{1,0:T(8,128)(2,1)} async-done(((bf16[40,1280]{1,0:T(8,128)(2,1)}), bf16[1280,1280]{1,0:T(8,128)(2,1)}) %all-gather.11.cloned.1.call-update) | async-done | bytes 3276816 | tf_op jit(solution)/shard_map/all_gather | solution.py:163
  280.7 3.4 %fusion.18 = bf16[128,1280]{1,0:T(8,128)(2,1)} fusion(f32[128,1280]{1,0:T(8,128)} %copy-done.2, bf16[128,1280]{0,1:T(8,128)(2,1)S(1)} %bitcast.72, bf16[1280,1280]{1,0:T(8,128)(2,1)} %all-gather.11.cloned.1.call-done, f32[1280]{0:T(1024)S(1)} %copy-done.8), kind=kOutput, calls=%fused_computation.27 | convolution fusion | flops 419921920 | bytes 4592640 | tf_op jit(solution)/shard_map/dot_general | solution.py:161
  (31 shorter events, 0.1 us)
Async XLA Ops:
  6.5 29.0 %copy-start = (bf16[1176,1280]{1,0:T(8,128)(2,1)S(1)}, bf16[1176,1280]{1,0:T(8,128)(2,1)}, u32[]{:S(2)}) copy-start(bf16[1176,1280]{1,0:T(8,128)(2,1)} %param.13) | copy-start | bytes 9031684
  6.5 111.7 %all-gather.5.cloned.1.call-start = ((), (), s32[]{:S(2)}) async-start(), calls=%async_computation.1 | async-start | bytes 10137600 | tf_op jit(solution)/shard_map/all_gather | solution.py:109
  9.4 25.0 %all-to-all-start = ((bf16[32,4,1176]{2,1,0:T(4,128)(2,1)}), bf16[32,4,1176]{2,1,0:T(4,128)(2,1)}, u32[]{:S(2)}, u32[]{:S(2)}) async-start(bf16[32,4,1176]{2,1,0:T(4,128)(2,1)} %all_to_all.8), calls=%async_computation | async-start | bytes 655360 | tf_op jit(solution)/shard_map/all_to_all | solution.py:97
  20.8 144.5 %all-gather.7.cloned.1.call-start = ((), (), s32[]{:S(2)}) async-start(), calls=%async_computation.2 | async-start | bytes 2949120 | tf_op jit(solution)/shard_map/all_gather | solution.py:140
  23.7 94.6 %copy-start.4 = (f32[1280]{0:T(1024)S(1)}, f32[1280]{0:T(1024)}, u32[]{:S(2)}) copy-start(f32[1280]{0:T(1024)} %param.15) | copy-start | bytes 15364
  23.7 94.6 %copy-start.5 = (f32[1280]{0:T(1024)S(1)}, f32[1280]{0:T(1024)}, u32[]{:S(2)}) copy-start(f32[1280]{0:T(1024)} %param.14) | copy-start | bytes 15364
  23.7 94.6 %copy-start.7 = (f32[3840]{0:T(1024)S(1)}, f32[3840]{0:T(1024)}, u32[]{:S(2)}) copy-start(f32[3840]{0:T(1024)} %param.17) | copy-start | bytes 46084
  36.2 0.9 copy-start.2
  123.8 1.3 copy-start.3
  137.4 59.1 %copy-start.6 = (s32[1,3]{1,0:T(1,128)S(1)}, s32[1,3]{1,0:T(1,128)}, u32[]{:S(2)}) copy-start(s32[1,3]{1,0:T(1,128)} %param.20) | copy-start | bytes 40
  140.3 56.1 %all-gather.9.cloned.1.call-start = ((), (), s32[]{:S(2)}) async-start(), calls=%async_computation.3 | async-start | bytes 2949120 | tf_op jit(solution)/shard_map/all_gather | solution.py:141
  142.2 138.4 %all-gather.11.cloned.1.call-start = ((), (), s32[]{:S(2)}) async-start(), calls=%async_computation.4 | async-start | bytes 3379200 | tf_op jit(solution)/shard_map/all_gather | solution.py:163
  196.5 84.2 %copy-start.8 = (f32[1280]{0:T(1024)S(1)}, f32[1280]{0:T(1024)}, u32[]{:S(2)}) copy-start(f32[1280]{0:T(1024)} %param.19) | copy-start | bytes 15364
  209.3 4.9 %copy-start.1 = (f32[16,512,128]{2,1,0:T(8,128)S(1)}, f32[16,512,128]{2,1,0:T(8,128)}, u32[]{:S(2)}) copy-start(f32[16,512,128]{2,1,0:T(8,128)} %get-tuple-element.395) | copy-start | bytes 12582916 | tf_op jit(solution)/shard_map/while
  228.1 5.0 %copy-start.1 = (f32[16,512,128]{2,1,0:T(8,128)S(1)}, f32[16,512,128]{2,1,0:T(8,128)}, u32[]{:S(2)}) copy-start(f32[16,512,128]{2,1,0:T(8,128)} %get-tuple-element.395) | copy-start | bytes 12582916 | tf_op jit(solution)/shard_map/while
Sparse Core Ops, SparseCore 0:
  10.0 108.2 all-gather.4
  140.4 24.8 all-gather.6
  167.2 29.2 all-gather.8
  198.9 81.7 all-gather.10
where the time goes:
time: 291 us
  waiting for transfers between devices  188 us (65%)
  local copies, waits for them, and re-layouts  38 us (13%)
  matrix products  28.1 us (10%)
  between operations  13.3 us (5%)
  starting transfers between devices  11.6 us (4%)
  other arithmetic  11.2 us (4%)
    all_gather x1, waiting for transfers between devices, per_device(): lax.all_gather(qkv_weight, 'dp', axis=0, tiled=True)  81 us
    all_gather x1, waiting for transfers between devices, per_device(): lax.all_gather(out_weight, 'dp', axis=0, tiled=True)  45.3 us
    all_gather x1, waiting for transfers between devices, per_device(): piece_values = lax.all_gather(values, 'seq', axis=0, tiled=True)  31.1 us
    all_gather x1, waiting for transfers between devices, per_device(): piece_keys = lax.all_gather(key_rows, 'seq', axis=0, tiled=True)  21.3 us
    dynamic_slice x4, local copies, waits for them, and re-layouts, one_block(): value_block = lax.dynamic_slice_in_dim(piece_values, first_row, length, 0)  11.8 us
    all_to_all x1, starting transfers between devices, per_device(): lax.all_to_all(pixels, 'dp', split_axis=0, concat_axis=0, tiled=True)  11.4 us
    dot_general x2, matrix products, attend_block(): jnp.einsum('hqk,khd->qhd', weights.astype(jnp.bfloat16), value_block.resh...  9.84 us
    dot_general x2, matrix products, attend_block(): jnp.einsum('qhd,khd->hqk', queries3, key_block.reshape(count, HEADS, HDIM...  8.54 us
  transfers between devices with their start and end apart: 5, of which 5 were waited for; matrix products, arithmetic and copies ran while one was open for 17% of the time, Pallas kernels for 0%

commit v1 on v0

--- a/solution.py
+++ b/solution.py
@@ -106,7 +106,9 @@
     projected = (
         jnp.dot(
             columns,
-            lax.all_gather(qkv_weight, "dp", axis=0, tiled=True),
+            jnp.concatenate(
+                lax.all_to_all(jnp.stack([qkv_weight] * lax.axis_size("dp")), "dp", 0, 0), axis=0
+            ),
             preferred_element_type=jnp.float32,
         )
         + qkv_bias

time: 291 us -> 446 us (1.53)
  waiting for transfers between devices: 188 us -> 319 us
  blocking collectives: 0 us -> 24.8 us
  starting transfers between devices: 11.6 us -> 5.24 us
  local copies, waits for them, and re-layouts: 38 us -> 44.2 us
    all_to_all x1, waiting for transfers between devices: 8.46 us -> 212 us  [per_device(): lax.all_to_all(jnp.stack([qkv_weight] * lax.axis_size('dp')), 'dp', 0, 0)]
    all_gather x1 -> x0, waiting for transfers between devices: 81 us -> none  [per_device(): lax.all_gather(qkv_weight, 'dp', axis=0, tiled=True)]
    all_to_all x0 -> x1, blocking collectives: none -> 24.8 us  [per_device(): lax.all_to_all(pixels, 'dp', split_axis=0, concat_axis=0, tiled=True)]
    all_gather x1, waiting for transfers between devices: 21.3 us -> 29.7 us  [per_device(): piece_keys = lax.all_gather(key_rows, 'seq', axis=0, tiled=True)]
    all_to_all x1, starting transfers between devices: 11.4 us -> 5.11 us  [per_device(): lax.all_to_all(jnp.stack([qkv_weight] * lax.axis_size('dp')), 'dp', 0, 0)]
    another operation x0 -> x1, local copies, waits for them, and re-layouts: none -> 5.37 us  [per_device(): jnp.stack([qkv_weight] * lax.axis_size('dp'))]
  transfers between devices with their start and end apart: 5 -> 4, of which waited for: 5 -> 4; matrix products, arithmetic and copies ran while one was open for 17% -> 10% of each run, Pallas kernels for 0% -> 0%
where the time goes in v1:
time: 446 us; the launch traced here: 445 us
  waiting for transfers between devices  319 us (72%)
  local copies, waits for them, and re-layouts  44.2 us (10%)
  matrix products  28.1 us (6%)
  blocking collectives  24.8 us (6%)
  between operations  13.3 us (3%)
  other arithmetic  9.9 us (2%)
  starting transfers between devices  5.24 us (1%)
    all_to_all x1, waiting for transfers between devices, per_device(): lax.all_to_all(jnp.stack([qkv_weight] * lax.axis_size('dp')), 'dp', 0, 0)  212 us
    all_gather x1, waiting for transfers between devices, per_device(): lax.all_gather(out_weight, 'dp', axis=0, tiled=True)  45.5 us
    all_gather x1, waiting for transfers between devices, per_device(): piece_values = lax.all_gather(values, 'seq', axis=0, tiled=True)  31.1 us
    all_gather x1, waiting for transfers between devices, per_device(): piece_keys = lax.all_gather(key_rows, 'seq', axis=0, tiled=True)  29.7 us
    all_to_all x1, blocking collectives, per_device(): lax.all_to_all(pixels, 'dp', split_axis=0, concat_axis=0, tiled=True)  24.8 us
    dynamic_slice x4, local copies, waits for them, and re-layouts, one_block(): value_block = lax.dynamic_slice_in_dim(piece_values, first_row, length, 0)  11.8 us
    dot_general x2, matrix products, attend_block(): jnp.einsum('hqk,khd->qhd', weights.astype(jnp.bfloat16), value_block.resh...  9.86 us
  transfers between devices with their start and end apart: 4, of which 4 were waited for; matrix products, arithmetic and copies ran while one was open for 10% of the time, Pallas kernels for 0%

profile of v1, /device:TPU:8, one launch (start us, length us, event | category | flops | bytes accessed | tf_op | source)
XLA Modules:
  0.0 444.7 jit_solution(385462956212304883)
XLA Ops:
  6.5 0.0 copy-start
  6.5 2.0 copy.27
  8.5 1.1 all_to_all.11
  9.6 24.8 %all_to_all.17 = bf16[32,4,1176]{2,1,0:T(4,128)(2,1)} all-to-all(bf16[32,4,1176]{2,1,0:T(4,128)(2,1)S(1)} %all_to_all.11), channel_id=1, replica_groups=mesh['dp'=32,'seq'=8] {'dp'}, dimensions={0} | all-to-all | bytes 602112 | tf_op jit(solution)/shard_map/all_to_all | solution.py:97
  34.4 5.4 %stack.2 = bf16[32,40,3840]{2,1,0:T(8,128)(2,1)} broadcast(bf16[40,3840]{1,0:T(8,128)(2,1)} %param.16), dimensions={1,2} | broadcast | bytes 10137600 | tf_op jit(solution)/shard_map/stack | solution.py:110
  39.8 5.1 %all-to-all-start.1 = ((bf16[32,40,3840]{2,1,0:T(8,128)(2,1)}), bf16[32,40,3840]{2,1,0:T(8,128)(2,1)}, u32[]{:S(2)}, u32[]{:S(2)}) async-start(bf16[32,40,3840]{2,1,0:T(8,128)(2,1)} %stack.2), calls=%async_computation.1 | async-start | bytes 19660800 | tf_op jit(solution)/shard_map/all_to_all | solution.py:110
  44.9 0.0 copy-start.4
  44.9 0.0 copy-start.5
  44.9 0.0 copy-start.7
  44.9 0.0 all-gather.4.cloned.1.call-start
  45.0 0.0 copy-done.6
  45.0 0.1 convert_reduce_fusion.1
  45.1 0.0 copy-done.9
  45.1 0.1 select_reduce_fusion.1
  45.2 0.1 fusion.26
  45.3 0.1 broadcast_multiply_fusion.1
  45.4 0.2 fusion.25
  45.6 0.9 mul.198
  46.5 2.2 copy.28
  48.6 1.1 all_to_all.13
  49.7 0.7 fusion.28
  50.5 0.8 copy-done.2
  51.3 0.2 multiply_reduce_fusion
  51.5 212.1 %all-to-all-done.1 = bf16[32,40,3840]{2,1,0:T(8,128)(2,1)} async-done(((bf16[32,40,3840]{2,1,0:T(8,128)(2,1)}), bf16[32,40,3840]{2,1,0:T(8,128)(2,1)}, u32[]{:S(2)}, u32[]{:S(2)}) %all-to-all-start.1) | async-done | bytes 9830432 | tf_op jit(solution)/shard_map/all_to_all | solution.py:110
  263.6 5.5 %convolution_add_fusion = f32[128,3840]{1,0:T(8,128)S(1)} fusion(bf16[1280,3840]{1,0:T(8,128)(2,1)} %bitcast.1, f32[3840]{0:T(1024)S(1)} %copy-done.7, f32[128,1280]{1,0:T(8,128)} %copy-done.2, f32[1280]{0:T(1024)S(1)} %copy-done.4, f32[1280]{0:T(1024)S(1)} %copy-done.5, f32[128]{0:T(128)S(1)} %add_rsqrt_fusion, f32[128]{0:T(128)S(1)} %broadcast_multiply_fusion.2), kind=kOutput, calls=%fused_computation.24 | convolution fusion | flops 1259601920 | bytes 12478464 | tf_op jit(solution)/shard_map/dot_general | solution.py:107
  269.2 1.3 copy-done.3
  270.5 1.2 fusion.27
  271.6 2.2 copy.29
  273.8 2.2 copy.32
  276.0 1.4 slice_negate_fusion
  277.3 1.1 maximum_multiply_fusion.1
  278.5 2.2 copy.30
  280.6 2.2 copy.33
  282.8 2.9 add_convert_fusion
  285.7 0.0 all-gather.4.cloned.1.call-update
  285.7 0.0 all-gather.6.cloned.1.call-start
  285.8 1.9 slice.41
  287.6 0.0 all-gather.6.cloned.1.call-update
  287.6 0.0 all-gather.8.cloned.1.call-start
  287.7 0.7 all-gather.8.cloned.1.call-update
  288.4 1.2 copy.34
  289.6 29.7 %all-gather.4.cloned.1.call-done = bf16[1024,1280]{1,0:T(8,128)(2,1)} async-done(((bf16[128,1280]{1,0:T(8,128)(2,1)}), bf16[1024,1280]{1,0:T(8,128)(2,1)}) %all-gather.4.cloned.1.call-update) | async-done | bytes 2621456 | tf_op jit(solution)/shard_map/all_gather | solution.py:142
  319.2 31.1 %all-gather.6.cloned.1.call-done = bf16[1024,1280]{1,0:T(8,128)(2,1)} async-done(((bf16[128,1280]{1,0:T(8,128)(2,1)}), bf16[1024,1280]{1,0:T(8,128)(2,1)}) %all-gather.6.cloned.1.call-update) | async-done | bytes 2621456 | tf_op jit(solution)/shard_map/all_gather | solution.py:143
  350.4 37.7 %while.20 = (s32[]{:T(128)}, f32[16,128]{1,0:T(8,128)S(1)}, f32[16,128]{1,0:T(8,128)S(1)}, f32[128,16,80]{0,2,1:T(8,128)}, s32[128]{0:T(128)S(1)}, /*index=5*/s3...) while((s32[]{:T(128)}, f32[16,128]{1,0:T(8,128)S(1)}, ...), condition=%wide.region_9.10_spmd.clone, body=%wide.region_5.9_spmd.clone.sunk | while | flops 349750272 | bytes 44511972 | solution.py:156
  350.4 3.5 constant_dynamic-slice_fusion.3
  353.8 2.4 copy.42
  356.3 0.1 convert_reduce_fusion.3
  356.4 0.1 broadcast_compare_fusion.2
  356.5 4.3 fusion.50
  360.8 2.4 copy.43
  363.2 4.9 %fusion.54 = f32[128,16,80]{0,2,1:T(8,128)} fusion(bf16[512,16,80]{0,2,1:T(8,128)(2,1)} %bitcast.66, f32[16,512,128]{2,1,0:T(8,128)} %get-tuple-element.395, f32[16,128]{1,0:T(8,128)S(1)} %get-tuple-element.425, pred[128,512]{0,1:T(8,128)(4,1)S(1)} %broadcast_compare_fusion.2, f32[128,16,80]{0,2,1:T(8,128)} %get-tuple-element.414, ...), kind=kOutput, calls=%fused_computation.8.clone.1 | convolution fusion | flops 173506560 | bytes 6897665 | tf_op jit(solution)/shard_map/while/body/eval_jaxpr/hqk,khd->qhd/dot_general | solution.py:75
  368.1 1.0 fusion.52
  369.1 3.5 constant_dynamic-slice_fusion.3
  372.6 2.4 copy.42
  375.0 0.1 convert_reduce_fusion.3
  375.1 0.1 broadcast_compare_fusion.2
  375.3 4.3 fusion.50
  379.6 2.4 copy.43
  382.0 5.0 %fusion.54 = f32[128,16,80]{0,2,1:T(8,128)} fusion(bf16[512,16,80]{0,2,1:T(8,128)(2,1)} %bitcast.66, f32[16,512,128]{2,1,0:T(8,128)} %get-tuple-element.395, f32[16,128]{1,0:T(8,128)S(1)} %get-tuple-element.425, pred[128,512]{0,1:T(8,128)(4,1)S(1)} %broadcast_compare_fusion.2, f32[128,16,80]{0,2,1:T(8,128)} %get-tuple-element.414, ...), kind=kOutput, calls=%fused_computation.8.clone.1 | convolution fusion | flops 173506560 | bytes 6897665 | tf_op jit(solution)/shard_map/while/body/eval_jaxpr/hqk,khd->qhd/dot_general | solution.py:75
  387.0 1.0 fusion.52
  388.1 1.1 divide_convert_fusion
  389.2 45.5 %all-gather.8.cloned.1.call-done = bf16[1280,1280]{1,0:T(8,128)(2,1)} async-done(((bf16[40,1280]{1,0:T(8,128)(2,1)}), bf16[1280,1280]{1,0:T(8,128)(2,1)}) %all-gather.8.cloned.1.call-update) | async-done | bytes 3276816 | tf_op jit(solution)/shard_map/all_gather | solution.py:165
  434.7 0.0 copy-done.8
  434.7 3.4 fusion.18
  (32 shorter events, 0.1 us)
Async XLA Ops:
  6.5 43.2 %copy-start = (bf16[1176,1280]{1,0:T(8,128)(2,1)S(1)}, bf16[1176,1280]{1,0:T(8,128)(2,1)}, u32[]{:S(2)}) copy-start(bf16[1176,1280]{1,0:T(8,128)(2,1)} %param.13) | copy-start | bytes 9031684
  39.8 5.2 %copy-start.6 = (s32[1,3]{1,0:T(1,128)S(1)}, s32[1,3]{1,0:T(1,128)}, u32[]{:S(2)}) copy-start(s32[1,3]{1,0:T(1,128)} %param.20) | copy-start | bytes 40
  39.8 5.3 %copy-start.9 = (s32[1,3]{1,0:T(1,128)S(1)}, s32[1,3]{1,0:T(1,128)}, u32[]{:S(2)}) copy-start(s32[1,3]{1,0:T(1,128)} %param.21) | copy-start | bytes 40
  39.8 223.8 %all-to-all-start.1 = ((bf16[32,40,3840]{2,1,0:T(8,128)(2,1)}), bf16[32,40,3840]{2,1,0:T(8,128)(2,1)}, u32[]{:S(2)}, u32[]{:S(2)}) async-start(bf16[32,40,3840]{2,1,0:T(8,128)(2,1)} %stack.2), calls=%async_computation.1 | async-start | bytes 19660800 | tf_op jit(solution)/shard_map/all_to_all | solution.py:110
  44.9 218.7 %copy-start.4 = (f32[1280]{0:T(1024)S(1)}, f32[1280]{0:T(1024)}, u32[]{:S(2)}) copy-start(f32[1280]{0:T(1024)} %param.15) | copy-start | bytes 15364
  44.9 218.7 %copy-start.5 = (f32[1280]{0:T(1024)S(1)}, f32[1280]{0:T(1024)}, u32[]{:S(2)}) copy-start(f32[1280]{0:T(1024)} %param.14) | copy-start | bytes 15364
  44.9 218.7 %copy-start.7 = (f32[3840]{0:T(1024)S(1)}, f32[3840]{0:T(1024)}, u32[]{:S(2)}) copy-start(f32[3840]{0:T(1024)} %param.17) | copy-start | bytes 46084
  44.9 274.3 %all-gather.4.cloned.1.call-start = ((), (), s32[]{:S(2)}) async-start(), calls=%async_computation.2 | async-start | bytes 2949120 | tf_op jit(solution)/shard_map/all_gather | solution.py:142
  50.4 0.8 copy-start.2
  269.2 1.3 copy-start.3
  285.7 64.7 %all-gather.6.cloned.1.call-start = ((), (), s32[]{:S(2)}) async-start(), calls=%async_computation.3 | async-start | bytes 2949120 | tf_op jit(solution)/shard_map/all_gather | solution.py:143
  287.6 147.1 %all-gather.8.cloned.1.call-start = ((), (), s32[]{:S(2)}) async-start(), calls=%async_computation.4 | async-start | bytes 3379200 | tf_op jit(solution)/shard_map/all_gather | solution.py:165
  350.4 84.4 %copy-start.8 = (f32[1280]{0:T(1024)S(1)}, f32[1280]{0:T(1024)}, u32[]{:S(2)}) copy-start(f32[1280]{0:T(1024)} %param.19) | copy-start | bytes 15364
  363.2 4.9 %copy-start.1 = (f32[16,512,128]{2,1,0:T(8,128)S(1)}, f32[16,512,128]{2,1,0:T(8,128)}, u32[]{:S(2)}) copy-start(f32[16,512,128]{2,1,0:T(8,128)} %get-tuple-element.395) | copy-start | bytes 12582916 | tf_op jit(solution)/shard_map/while
  382.0 5.0 %copy-start.1 = (f32[16,512,128]{2,1,0:T(8,128)S(1)}, f32[16,512,128]{2,1,0:T(8,128)}, u32[]{:S(2)}) copy-start(f32[16,512,128]{2,1,0:T(8,128)} %get-tuple-element.395) | copy-start | bytes 12582916 | tf_op jit(solution)/shard_map/while
Sparse Core Ops, SparseCore 0:
  285.8 33.3 all-gather.3
  321.1 29.2 all-gather.5
  353.0 81.7 all-gather.7
